TPU v7x, 32 devices: a whole 2x2x4 slice. The times are simulated.
32 devices in a mesh: groups: 2 (over x), blk: 16 (over z, y, core).
Axes of the slice: x: 2, y: 2, z: 4, core: 2. Of those that a mesh axis runs over, the one named last changes fastest.
Arguments:
- queries: bfloat16 [32, 8192], P(('groups', 'blk')), parts along dimension 0, may hold values from -13 to 13
- cache_keys: bfloat16 [8192, 1024], P(('groups', 'blk')), parts along dimension 0, may hold values from -10 to 10
- cache_values: bfloat16 [8192, 1024], P(('groups', 'blk')), parts along dimension 0, may hold values from -5 to 5
- lengths: int32 [32], P(('groups', 'blk')), parts along dimension 0, may hold values from 1 to 256, as said below
- stretch_start: int32 [2], P('groups'), parts along dimension 0, may hold values from 2048 to 4080
- residual: float32 [32, 8192], P(('groups', 'blk')), parts along dimension 0, may hold values from -40 to 40
- out_weight: bfloat16 [8192, 8192], P('blk'), may hold values from -0.0625 to 0.0625
- norm_gain: float32 [8192], replicated, may hold values from 0.25 to 1.75
- gate_weight: bfloat16 [8192, 16384], P(None, 'blk'), may hold values from -0.0625 to 0.0625
- up_weight: bfloat16 [8192, 16384], P(None, 'blk'), may hold values from -0.0625 to 0.0625
- down_weight: bfloat16 [16384, 8192], P('blk'), may hold values from -0.046875 to 0.046875
Outputs:
- layer_out: float32 [32, 8192], P(('groups', 'blk')), parts along dimension 0
There are 2 independent parts, one for each index of `groups`. A program takes and returns all parts, laid end to end along the dimension named above; an argument that names none is the same for every part. Nothing has to cross between parts.
Inputs may be any that keep to these rules, and one draw needn't show every extreme that they name: `lengths`: each shard holds 1 to 256 live slots, and some shard is full.
All inputs are finite; a program needn't handle non-finite values.
Results may differ from a plain program's by a relative error of at most 0.0025.
Values may be sent and summed in bfloat16 or wider, within the bound.
A program may use at most 128 MiB of HBM per device.

v0:
```python
import jax
import jax.numpy as jnp
from jax import lax
from jax.sharding import PartitionSpec as P

QUERY_HEADS = 64
KV_HEADS = 8
HEAD_DIM = 128
NEG_FLOOR = -1e30
EPSILON = 1e-05


def body(
    queries,
    cache_keys,
    cache_values,
    lengths,
    stretch_start,
    residual,
    out_weight,
    norm_gain,
    gate_weight,
    up_weight,
    down_weight,
):
    group_size = QUERY_HEADS // KV_HEADS
    score_scale = HEAD_DIM ** (-0.5)
    span = group_size * HEAD_DIM
    all_queries = lax.all_gather(queries, "blk", axis=0, tiled=True)
    row_count = all_queries.shape[0]
    shard_len = cache_keys.shape[0]
    device = lax.axis_index("blk")
    slot_index = jnp.arange(shard_len, dtype=jnp.int32)
    position = device * shard_len + slot_index
    row_position = stretch_start[0] + jnp.arange(row_count, dtype=jnp.int32)
    visible = (slot_index[None, :] < lengths[0]) & (position[None, :] <= row_position[:, None])
    masked = visible[:, None, :]

    def head_step(head_index, state_in):
        numer_all, denom_all, peak_all = state_in
        q_block = lax.dynamic_slice_in_dim(all_queries, head_index * span, span, 1).reshape(
            row_count, group_size, HEAD_DIM
        )
        k_block = lax.dynamic_slice_in_dim(cache_keys, head_index * HEAD_DIM, HEAD_DIM, 1)
        v_block = lax.dynamic_slice_in_dim(cache_values, head_index * HEAD_DIM, HEAD_DIM, 1)
        scores = (
            jnp.einsum("rgd,kd->rgk", q_block, k_block, preferred_element_type=jnp.float32)
            * score_scale
        )
        local_max = jnp.max(jnp.where(masked, scores, NEG_FLOOR), axis=-1)
        weights = jnp.where(masked, jnp.exp(scores - local_max[:, :, None]), 0.0).astype(
            jnp.bfloat16
        )
        partial_out = jnp.einsum(
            "rgk,kd->rgd", weights, v_block, preferred_element_type=jnp.float32
        )
        partial_den = jnp.sum(weights, axis=-1, dtype=jnp.float32)
        numer_all = lax.dynamic_update_slice_in_dim(
            numer_all, partial_out.reshape(row_count, span), head_index * span, 1
        )
        denom_all = lax.dynamic_update_slice_in_dim(
            denom_all, partial_den, head_index * group_size, 1
        )
        peak_all = lax.dynamic_update_slice_in_dim(peak_all, local_max, head_index * group_size, 1)
        return (numer_all, denom_all, peak_all)

    start_state = (
        jnp.zeros((row_count, QUERY_HEADS * HEAD_DIM), jnp.float32),
        jnp.zeros((row_count, QUERY_HEADS), jnp.float32),
        jnp.zeros((row_count, QUERY_HEADS), jnp.float32),
    )
    numer_all, denom_all, peak_all = lax.fori_loop(0, KV_HEADS, head_step, start_state)
    global_max = lax.pmax(peak_all.astype(jnp.bfloat16), "blk").astype(peak_all.dtype)
    factor = jnp.exp(peak_all - global_max)
    scaled = (numer_all.reshape(row_count, QUERY_HEADS, HEAD_DIM) * factor[:, :, None]).reshape(
        row_count, QUERY_HEADS * HEAD_DIM
    )
    scaled_den = denom_all * factor
    numerator = lax.psum_scatter(scaled, "blk", scatter_dimension=1, tiled=True)
    denominator = lax.psum(scaled_den, "blk")
    col_count = numerator.shape[1]
    head_of = (device * col_count + jnp.arange(col_count, dtype=jnp.int32)) // HEAD_DIM
    head_pick = (jnp.arange(QUERY_HEADS, dtype=jnp.int32)[:, None] == head_of[None, :]).astype(
        jnp.float32
    )
    den_cols = jnp.dot(denominator, head_pick, precision=lax.Precision.HIGHEST)
    attn_cols = (numerator / den_cols).astype(jnp.bfloat16)
    picked = attn_cols
    attn_out = lax.psum_scatter(
        jnp.dot(picked, out_weight, preferred_element_type=jnp.float32),
        "blk",
        scatter_dimension=0,
        tiled=True,
    )
    mixed = residual + attn_out
    normed = (
        mixed * lax.rsqrt(jnp.mean(mixed * mixed, axis=-1, keepdims=True) + EPSILON) * norm_gain
    ).astype(jnp.bfloat16)
    row_piece = lax.all_gather(normed, "blk", axis=0, tiled=True)
    gate_term = jnp.dot(row_piece, gate_weight, preferred_element_type=jnp.float32)
    up_term = jnp.dot(row_piece, up_weight, preferred_element_type=jnp.float32)
    hidden_act = (jax.nn.silu(gate_term) * up_term).astype(jnp.bfloat16)
    picked = hidden_act
    ffn_out = lax.psum_scatter(
        jnp.dot(picked, down_weight, preferred_element_type=jnp.float32),
        "blk",
        scatter_dimension=0,
        tiled=True,
    )
    return mixed + ffn_out


def solution(mesh):
    in_specs = (
        P(("groups", "blk"), None),
        P(("groups", "blk"), None),
        P(("groups", "blk"), None),
        P(("groups", "blk")),
        P("groups"),
        P(("groups", "blk"), None),
        P("blk", None),
        P(),
        P(None, "blk"),
        P(None, "blk"),
        P("blk", None),
    )
    out_specs = P(("groups", "blk"), None)
    return jax.shard_map(body, mesh=mesh, in_specs=in_specs, out_specs=out_specs, check_vma=False)
```

profile of v0, /device:TPU:1, one launch (start us, length us, event | category | flops | bytes accessed | tf_op | source)
XLA Modules:
  0.0 380.7 jit_solution(13834208588220643452)
XLA Ops:
  6.5 24.8 %all-gather = bf16[16,1,8192]{2,1,0:T(2,128)(2,1)S(1)} all-gather(bf16[1,1,8192]{2,1,0:T(2,128)(2,1)} %bitcast.64), channel_id=1, replica_groups=mesh['groups'=2,'blk'=16] {'blk'}, dimensions={0}, use_global_device_ids=true | all-gather | bytes 278528 | tf_op jit(solution)/shard_map/all_gather | solution.py:29
  33.1 24.0 %while.18 = (s32[]{:T(128)}, f32[16,8192]{1,0:T(8,128)S(1)}, f32[16,64]{1,0:T(8,128)S(1)}, f32[16,64]{1,0:T(8,128)S(1)}, bf16[16,8192]{1,0:T(8,128)(2,1)S(1)}, /...) while((s32[]{:T(128)}, f32[16,8192]{1,0:T(8,128)S(1)}, ...), condition=%wide.region_3.4_spmd.clone, body=%wide.region_0.3_spmd.clone.sunk | while | flops 17145608 | bytes 906879 | solution.py:72
  33.2 1.1 select_reduce_fusion.2
  34.3 1.1 fusion.45
  36.1 1.1 select_reduce_fusion.2
  37.2 1.1 fusion.45
  39.2 1.1 select_reduce_fusion.2
  40.2 1.1 fusion.45
  42.2 1.1 select_reduce_fusion.2
  43.2 1.1 fusion.45
  45.2 1.1 select_reduce_fusion.2
  46.3 1.1 fusion.45
  48.2 1.1 select_reduce_fusion.2
  49.3 1.1 fusion.45
  51.2 1.1 select_reduce_fusion.2
  52.3 1.1 fusion.45
  54.2 1.1 select_reduce_fusion.2
  55.3 1.1 fusion.45
  57.1 29.0 %pmax.7 = bf16[16,64]{1,0:T(8,128)(2,1)S(1)} all-reduce(bf16[16,64]{1,0:T(8,128)(2,1)S(1)} %convert_element_type.30), channel_id=1, replica_groups=mesh['groups'=2,'blk'=16] {'blk'}, use_global_device_ids=true, to_apply=%region_4.5 | all-reduce | flops 1024 | bytes 4096 | tf_op jit(solution)/shard_map/pmax | solution.py:73
  86.3 1.1 bitcast_multiply_fusion
  87.6 30.3 %psum.7 = f32[16,64]{1,0:T(8,128)S(1)} all-reduce(f32[16,64]{1,0:T(8,128)S(1)} %get-tuple-element.196), channel_id=1, replica_groups=mesh['groups'=2,'blk'=16] {'blk'}, use_global_device_ids=true, to_apply=%region_6.7 | all-reduce | flops 1024 | bytes 8192 | tf_op jit(solution)/shard_map/psum | solution.py:80
  117.9 21.2 %reduce-scatter.2.cloned.1.call-done = f32[16,512]{1,0:T(8,128)} async-done(((f32[16,8192]{1,0:T(8,128)}), f32[16,512]{1,0:T(8,128)}) %reduce-scatter.2.cloned.1.call-update) | async-done | bytes 32784 | tf_op jit(solution)/shard_map/reduce_scatter | solution.py:79
  139.1 0.9 fusion.11
  140.0 5.4 %fusion.32 = f32[16,8192]{1,0:T(8,128)} fusion(bf16[16,512]{1,0:T(8,128)(2,1)S(1)} %fusion.11, bf16[512,8192]{1,0:T(8,128)(2,1)} %param.19), kind=kOutput, calls=%fused_computation.55 | convolution fusion | flops 134217728 | bytes 8929280 | tf_op jit(solution)/shard_map/dot_general | solution.py:90
  145.5 0.7 dynamic-slice
  146.2 91.0 %all-reduce.5.cloned.1.call-done = f32[16,8192]{1,0:T(8,128)} async-done(((f32[16,8192]{1,0:T(8,128)}), f32[16,8192]{1,0:T(8,128)}) %all-reduce.5.cloned.1.call-update) | async-done | bytes 524304
  237.2 2.3 multiply_reduce_fusion
  240.3 22.2 %all-gather.1 = bf16[16,1,8192]{2,1,0:T(2,128)(2,1)S(1)} all-gather(bf16[1,1,8192]{2,1,0:T(2,128)(2,1)S(1)} %convert_bitcast_fusion), channel_id=1, replica_groups=mesh['groups'=2,'blk'=16] {'blk'}, dimensions={0}, use_global_device_ids=true | all-gather | bytes 278528 | tf_op jit(solution)/shard_map/all_gather | solution.py:99
  262.5 8.0 %fusion.15 = f32[16,1024]{1,0:T(8,128)S(1)} fusion(bf16[8192,1024]{1,0:T(8,128)(2,1)} %param.21, bf16[16,1,8192]{2,1,0:T(2,128)(2,1)S(1)} %all-gather.1), kind=kOutput, calls=%fused_computation.23 | convolution fusion | flops 268435456 | bytes 17104896 | tf_op jit(solution)/shard_map/dot_general | solution.py:100
  270.5 13.7 %fusion.12 = f32[16,8192]{1,0:T(8,128)} fusion(bf16[1024,8192]{1,0:T(8,128)(2,1)} %param.23, bf16[8192,1024]{1,0:T(8,128)(2,1)} %param.22, bf16[16,1,8192]{2,1,0:T(2,128)(2,1)S(1)} %all-gather.1, f32[16,1024]{1,0:T(8,128)S(1)} %fusion.15), kind=kOutput, calls=%fused_computation.20 | convolution fusion | flops 536969216 | bytes 34406400 | tf_op jit(solution)/shard_map/dot_general | solution.py:105
  284.3 87.7 %all-reduce.7.cloned.1.call-done = f32[16,8192]{1,0:T(8,128)} async-done(((f32[16,8192]{1,0:T(8,128)}), f32[16,8192]{1,0:T(8,128)}) %all-reduce.7.cloned.1.call-update) | async-done | bytes 524304
  371.9 2.3 dynamic-slice_add_fusion
  (80 shorter events, 7.2 us)
Async XLA Ops:
  6.5 139.0 %copy-start.2 = (u32[32]{0:T(128)S(1)}, u32[32]{0:T(128)}, u32[]{:S(2)}) copy-start(u32[32]{0:T(128)} %constant.115) | copy-start | bytes 388
  6.5 230.7 %copy-start = (f32[1,8192]{1,0:T(1,128)S(1)}, f32[1,8192]{1,0:T(1,128)}, u32[]{:S(2)}) copy-start(f32[1,8192]{1,0:T(1,128)} %param.18) | copy-start | bytes 98308
  6.5 233.7 %copy-start.1 = (f32[8192]{0:T(1024)S(1)}, f32[8192]{0:T(1024)}, u32[]{:S(2)}) copy-start(f32[8192]{0:T(1024)} %param.20) | copy-start | bytes 98308
  6.5 132.6 %reduce-scatter.2.cloned.1.call-start = ((), (), s32[]{:S(2)}) async-start(), calls=%async_computation.1 | async-start | bytes 557056 | tf_op jit(solution)/shard_map/reduce_scatter | solution.py:79
  87.5 149.7 %all-reduce.5.cloned.1.call-start = ((), (), s32[]{:S(2)}) async-start(), calls=%async_computation.2 | async-start | bytes 1048576
  145.5 226.4 %all-reduce.7.cloned.1.call-start = ((), (), s32[]{:S(2)}) async-start(), calls=%async_computation.3 | async-start | bytes 1048576
Sparse Core Ops, SparseCore 0:
  87.6 51.4 reduce-scatter.1
  145.6 91.5 all-reduce.4
  284.4 87.4 all-reduce.6
where the time goes:
time: 382 us; the launch traced here: 381 us
  waiting for transfers between devices  200 us (52%)
  blocking collectives  106 us (28%)
  matrix products  45.2 us (12%)
  between operations  15.2 us (4%)
  other arithmetic  7.81 us (2%)
  local copies, waits for them, and re-layouts  5.68 us (1%)
    unnamed x5, waiting for transfers between devices  179 us
    psum x1, blocking collectives, body(): denominator = lax.psum(scaled_den, 'blk')  30.3 us
    pmax x1, blocking collectives, body(): lax.pmax(peak_all.astype(jnp.bfloat16), 'blk').astype(peak_all.dtype)  29 us
    all_gather x1, blocking collectives, body(): all_queries = lax.all_gather(queries, 'blk', axis=0, tiled=True)  24.8 us
    all_gather x1, blocking collectives, body(): row_piece = lax.all_gather(normed, 'blk', axis=0, tiled=True)  22.2 us
    reduce_scatter x1, waiting for transfers between devices, body(): numerator = lax.psum_scatter(scaled, 'blk', scatter_dimension=1, tiled=True)  21.2 us
    dot_general x1, matrix products, body(): jnp.dot(picked, down_weight, preferred_element_type=jnp.float32)  13.7 us
    dot_general x8, matrix products, head_step(): jnp.einsum('rgd,kd->rgk', q_block, k_block, preferred_element_type=jnp.fl...  8.7 us
  transfers between devices with their start and end apart: 3, of which 3 were waited for; matrix products, arithmetic and copies ran while one was open for 0% of the time, Pallas kernels for 0%

commit v1 on v0

--- a/solution.py
+++ b/solution.py
@@ -77,7 +77,7 @@
     )
     scaled_den = denom_all * factor
     numerator = lax.psum_scatter(scaled, "blk", scatter_dimension=1, tiled=True)
-    denominator = lax.psum(scaled_den, "blk")
+    denominator = jnp.sum(lax.all_gather(scaled_den, "blk"), axis=0)
     col_count = numerator.shape[1]
     head_of = (device * col_count + jnp.arange(col_count, dtype=jnp.int32)) // HEAD_DIM
     head_pick = (jnp.arange(QUERY_HEADS, dtype=jnp.int32)[:, None] == head_of[None, :]).astype(

time: 382 us -> 382 us (level)
  waiting for transfers between devices: 200 us -> 212 us
  blocking collectives: 106 us -> 94.3 us
    psum x1 -> x0, blocking collectives: 30.3 us -> none  [body(): denominator = lax.psum(scaled_den, 'blk')]
    all_gather x0 -> x1, blocking collectives: none -> 18.3 us  [body(): denominator = jnp.sum(lax.all_gather(scaled_den, 'blk'), axis=0)]
    reduce_scatter x1, waiting for transfers between devices: 21.2 us -> 33.2 us  [body(): numerator = lax.psum_scatter(scaled, 'blk', scatter_dimension=1, tiled=True)]
where the time goes in v1:
time: 382 us; the launch traced here: 381 us
  waiting for transfers between devices  212 us (55%)
  blocking collectives  94.3 us (25%)
  matrix products  45.2 us (12%)
  between operations  15.2 us (4%)
  other arithmetic  7.83 us (2%)
  local copies, waits for them, and re-layouts  5.68 us (1%)
    unnamed x5, waiting for transfers between devices  179 us
    reduce_scatter x1, waiting for transfers between devices, body(): numerator = lax.psum_scatter(scaled, 'blk', scatter_dimension=1, tiled=True)  33.2 us
    pmax x1, blocking collectives, body(): lax.pmax(peak_all.astype(jnp.bfloat16), 'blk').astype(peak_all.dtype)  29 us
    all_gather x1, blocking collectives, body(): all_queries = lax.all_gather(queries, 'blk', axis=0, tiled=True)  24.8 us
    all_gather x1, blocking collectives, body(): row_piece = lax.all_gather(normed, 'blk', axis=0, tiled=True)  22.2 us
    all_gather x1, blocking collectives, body(): denominator = jnp.sum(lax.all_gather(scaled_den, 'blk'), axis=0)  18.3 us
    dot_general x1, matrix products, body(): jnp.dot(picked, down_weight, preferred_element_type=jnp.float32)  13.7 us
    dot_general x8, matrix products, head_step(): jnp.einsum('rgd,kd->rgk', q_block, k_block, preferred_element_type=jnp.fl...  8.7 us
  transfers between devices with their start and end apart: 3, of which 3 were waited for; matrix products, arithmetic and copies ran while one was open for 0% of the time, Pallas kernels for 0%

profile of v1, /device:TPU:1, one launch (start us, length us, event | category | flops | bytes accessed | tf_op | source)
XLA Modules:
  0.0 380.7 jit_solution(13739207883662288507)
XLA Ops:
  6.5 24.8 %all-gather.1 = bf16[16,1,8192]{2,1,0:T(2,128)(2,1)S(1)} all-gather(bf16[1,1,8192]{2,1,0:T(2,128)(2,1)} %bitcast.66), channel_id=1, replica_groups=mesh['groups'=2,'blk'=16] {'blk'}, dimensions={0}, use_global_device_ids=true | all-gather | bytes 278528 | tf_op jit(solution)/shard_map/all_gather | solution.py:29
  33.1 24.0 %while.18 = (s32[]{:T(128)}, f32[16,8192]{1,0:T(8,128)S(1)}, f32[16,64]{1,0:T(8,128)S(1)}, f32[16,64]{1,0:T(8,128)S(1)}, bf16[16,8192]{1,0:T(8,128)(2,1)S(1)}, /...) while((s32[]{:T(128)}, f32[16,8192]{1,0:T(8,128)S(1)}, ...), condition=%wide.region_3.4_spmd.clone, body=%wide.region_0.3_spmd.clone.sunk | while | flops 17145608 | bytes 906879 | solution.py:72
  33.2 1.1 select_reduce_fusion.2
  34.3 1.1 fusion.45
  36.1 1.1 select_reduce_fusion.2
  37.2 1.1 fusion.45
  39.2 1.1 select_reduce_fusion.2
  40.2 1.1 fusion.45
  42.2 1.1 select_reduce_fusion.2
  43.2 1.1 fusion.45
  45.2 1.1 select_reduce_fusion.2
  46.3 1.1 fusion.45
  48.2 1.1 select_reduce_fusion.2
  49.3 1.1 fusion.45
  51.2 1.1 select_reduce_fusion.2
  52.3 1.1 fusion.45
  54.2 1.1 select_reduce_fusion.2
  55.3 1.1 fusion.45
  57.1 29.0 %pmax.7 = bf16[16,64]{1,0:T(8,128)(2,1)S(1)} all-reduce(bf16[16,64]{1,0:T(8,128)(2,1)S(1)} %convert_element_type.30), channel_id=1, replica_groups=mesh['groups'=2,'blk'=16] {'blk'}, use_global_device_ids=true, to_apply=%region_4.5 | all-reduce | flops 1024 | bytes 4096 | tf_op jit(solution)/shard_map/pmax | solution.py:73
  86.3 1.1 bitcast_multiply_fusion
  87.6 18.3 %all-gather = f32[256,64]{1,0:T(8,128)S(1)} all-gather(f32[16,64]{1,0:T(8,128)S(1)} %get-tuple-element.196), channel_id=2, replica_groups=mesh['groups'=2,'blk'=16] {'blk'}, dimensions={0}, use_global_device_ids=true | all-gather | bytes 69632 | tf_op jit(solution)/shard_map/all_gather | solution.py:80
  105.9 33.2 %reduce-scatter.2.cloned.1.call-done = f32[16,512]{1,0:T(8,128)} async-done(((f32[16,8192]{1,0:T(8,128)}), f32[16,512]{1,0:T(8,128)}) %reduce-scatter.2.cloned.1.call-update) | async-done | bytes 32784 | tf_op jit(solution)/shard_map/reduce_scatter | solution.py:79
  139.1 0.9 fusion.11
  140.0 5.4 %fusion.32 = f32[16,8192]{1,0:T(8,128)} fusion(bf16[16,512]{1,0:T(8,128)(2,1)S(1)} %fusion.11, bf16[512,8192]{1,0:T(8,128)(2,1)} %param.19), kind=kOutput, calls=%fused_computation.55 | convolution fusion | flops 134217728 | bytes 8929280 | tf_op jit(solution)/shard_map/dot_general | solution.py:90
  145.5 0.7 dynamic-slice
  146.2 91.0 %all-reduce.5.cloned.1.call-done = f32[16,8192]{1,0:T(8,128)} async-done(((f32[16,8192]{1,0:T(8,128)}), f32[16,8192]{1,0:T(8,128)}) %all-reduce.5.cloned.1.call-update) | async-done | bytes 524304
  237.2 2.3 multiply_reduce_fusion
  240.3 22.2 %all-gather.2 = bf16[16,1,8192]{2,1,0:T(2,128)(2,1)S(1)} all-gather(bf16[1,1,8192]{2,1,0:T(2,128)(2,1)S(1)} %convert_bitcast_fusion), channel_id=1, replica_groups=mesh['groups'=2,'blk'=16] {'blk'}, dimensions={0}, use_global_device_ids=true | all-gather | bytes 278528 | tf_op jit(solution)/shard_map/all_gather | solution.py:99
  262.5 8.0 %fusion.15 = f32[16,1024]{1,0:T(8,128)S(1)} fusion(bf16[8192,1024]{1,0:T(8,128)(2,1)} %param.21, bf16[16,1,8192]{2,1,0:T(2,128)(2,1)S(1)} %all-gather.2), kind=kOutput, calls=%fused_computation.23 | convolution fusion | flops 268435456 | bytes 17104896 | tf_op jit(solution)/shard_map/dot_general | solution.py:100
  270.5 13.7 %fusion.12 = f32[16,8192]{1,0:T(8,128)} fusion(bf16[1024,8192]{1,0:T(8,128)(2,1)} %param.23, bf16[8192,1024]{1,0:T(8,128)(2,1)} %param.22, bf16[16,1,8192]{2,1,0:T(2,128)(2,1)S(1)} %all-gather.2, f32[16,1024]{1,0:T(8,128)S(1)} %fusion.15), kind=kOutput, calls=%fused_computation.20 | convolution fusion | flops 536969216 | bytes 34406400 | tf_op jit(solution)/shard_map/dot_general | solution.py:105
  284.3 87.7 %all-reduce.7.cloned.1.call-done = f32[16,8192]{1,0:T(8,128)} async-done(((f32[16,8192]{1,0:T(8,128)}), f32[16,8192]{1,0:T(8,128)}) %all-reduce.7.cloned.1.call-update) | async-done | bytes 524304
  371.9 2.3 dynamic-slice_add_fusion
  (81 shorter events, 7.2 us)
Async XLA Ops:
  6.5 139.0 %copy-start.2 = (u32[32]{0:T(128)S(1)}, u32[32]{0:T(128)}, u32[]{:S(2)}) copy-start(u32[32]{0:T(128)} %constant.115) | copy-start | bytes 388
  6.5 230.7 %copy-start = (f32[1,8192]{1,0:T(1,128)S(1)}, f32[1,8192]{1,0:T(1,128)}, u32[]{:S(2)}) copy-start(f32[1,8192]{1,0:T(1,128)} %param.18) | copy-start | bytes 98308
  6.5 233.7 %copy-start.1 = (f32[8192]{0:T(1024)S(1)}, f32[8192]{0:T(1024)}, u32[]{:S(2)}) copy-start(f32[8192]{0:T(1024)} %param.20) | copy-start | bytes 98308
  6.5 132.6 %reduce-scatter.2.cloned.1.call-start = ((), (), s32[]{:S(2)}) async-start(), calls=%async_computation.1 | async-start | bytes 557056 | tf_op jit(solution)/shard_map/reduce_scatter | solution.py:79
  87.5 149.7 %all-reduce.5.cloned.1.call-start = ((), (), s32[]{:S(2)}) async-start(), calls=%async_computation.2 | async-start | bytes 1048576
  145.5 226.4 %all-reduce.7.cloned.1.call-start = ((), (), s32[]{:S(2)}) async-start(), calls=%async_computation.3 | async-start | bytes 1048576
Sparse Core Ops, SparseCore 0:
  87.6 51.4 reduce-scatter.1
  145.6 91.5 all-reduce.4
  284.4 87.4 all-reduce.6
